TPU v7x, 512 devices: a whole 4x4x16 slice. The times are simulated.
512 devices in a mesh: blk: 64 (over z, y), pslab: 8 (over x, core).
Axes of the slice: x: 4, y: 4, z: 16, core: 2. Of those that a mesh axis runs over, the one named last changes fastest.
Arguments:
- positions: float32 [64, 8, 64, 512], P('blk', 'pslab'), may hold values from 0 to 32768
- masses: bfloat16 [64, 8, 64, 512], P('blk', 'pslab'), may hold values from -6 to 6
- send_counts: int32 [64, 8, 64], P('blk', 'pslab'), may hold values from 0 to 512, as said below
- legendre: bfloat16 [16384, 64, 128], P(('pslab', 'blk')), may hold values from -0.75 to 0.75
- cycle_order: int32 [64], replicated, may hold values from 0 to 63, each once
- m_order: int32 [16384], replicated, may hold values from 0 to 16383, each once
Outputs:
- alm: float32 [16384, 2, 128], P(('pslab', 'blk'))
Inputs may be any that keep to these rules, and one draw needn't show every extreme that they name: `send_counts`: live slots from one device to one owner are at most 512; in every draw one owner gets 512 from every device. `cycle_order`: a permutation of the cycles. `m_order`: a permutation of the orders.
All inputs are finite; a program needn't handle non-finite values.
Results may differ from a plain program's by a relative error of at most 0.004.
Values may be sent and summed in bfloat16 or wider, within the bound.
No kernel may reach another device: no remote copies, remote signals or barrier semaphores. Data moves between devices by JAX's collectives and lax.ppermute only.
A program may use at most 64 MiB of HBM per device.

v0:
```python
import math

import jax
import jax.numpy as jnp
import numpy as np
from jax import lax
from jax.experimental import pallas as pl
from jax.experimental.pallas import tpu as pltpu
from jax.sharding import PartitionSpec as P

CYCLE_LEN = 32768
M = 16384
LMAX = 16384
LW = 128

LANES = 128
ROWS = CYCLE_LEN // LANES
UPPER = M // ROWS
TILES = 8
SUB = LANES // TILES
COLUMNS = (TILES + 1) * SUB

FIRST_IN_BLOCK = 18
FIRST_ON_LINE = 16
FIRST_IN_PLANE = 9

F32 = jnp.float32
BF16 = jnp.bfloat16

NT = (((1,), (1,)), ((), ()))
NN = (((1,), (0,)), ((), ()))


def halves(table):
    high = table.astype(jnp.bfloat16)
    low = (table - high.astype(np.float64)).astype(jnp.bfloat16)
    return high, low


def split(values):
    high = values.astype(BF16)
    low = (values - high.astype(F32)).astype(BF16)
    return high, low


def tables():
    two_pi = 2.0 * math.pi
    rows = np.arange(ROWS)
    lanes = np.arange(LANES)
    lanes = TILES * (lanes % SUB) + lanes // SUB
    upper = np.arange(UPPER)
    angle_one = (rows[:, None] * rows[None, :] % ROWS) * (two_pi / ROWS)
    one = np.concatenate([np.cos(angle_one), -np.sin(angle_one)], axis=0)
    twist = (rows[:, None] * lanes[None, :] % CYCLE_LEN) * (two_pi / CYCLE_LEN)
    angle_two = (upper[:, None] * lanes[None, :] % LANES) * (two_pi / LANES)
    cos_two, sin_two = np.cos(angle_two), np.sin(angle_two)
    two = np.concatenate(
        [
            np.concatenate([cos_two, sin_two], axis=1),
            np.concatenate([-sin_two, cos_two], axis=1),
        ],
        axis=0,
    ) * (CYCLE_LEN ** -0.5)
    return (
        *halves(one),
        np.cos(twist).astype(np.float32),
        np.sin(twist).astype(np.float32),
        *halves(two),
    )


def spread_row(values, row, count):
    tile = jnp.broadcast_to(values[row : row + 1, :], (16, LANES)).astype(BF16)
    return jnp.concatenate([tile] * (count // 16), axis=0)


def row_ids(count):
    return lax.broadcasted_iota(jnp.int32, (count, LANES), 0).astype(F32).astype(BF16)


def pack_kernel(positions_hbm, masses_hbm, counts_hbm, out_hbm, positions_ref, masses_ref, counts_ref, out_ref, sems):
    owners, capacity = positions_ref.shape
    rows = 16
    chunks = owners // rows
    in_copies, out_copies = [], []
    for n in range(chunks):
        part = pl.ds(n * rows, rows)
        in_copies.append(
            (
                pltpu.make_async_copy(positions_hbm.at[part, :], positions_ref.at[part, :], sems.at[n, 0]),
                pltpu.make_async_copy(masses_hbm.at[part, :], masses_ref.at[part, :], sems.at[n, 1]),
            )
        )
        cuts = sorted({n * rows, min(max(FIRST_IN_BLOCK, n * rows), (n + 1) * rows), (n + 1) * rows})
        out_copies.append(
            [
                pltpu.make_async_copy(
                    out_ref.at[pl.ds(8 * a, 8 * (b - a)), :],
                    out_hbm.at[pl.ds(8 * ((a - FIRST_IN_BLOCK) % owners), 8 * (b - a)), :],
                    sems.at[n, 2 + m],
                )
                for m, (a, b) in enumerate(zip(cuts, cuts[1:]))
            ]
        )
    counts_copy = pltpu.make_async_copy(counts_hbm, counts_ref, sems.at[chunks, 0])
    counts_copy.start()
    for copies in in_copies:
        for copy in copies:
            copy.start()
    counts_copy.wait()
    row = lax.broadcasted_iota(jnp.int32, (owners, owners), 0)
    column = lax.broadcasted_iota(jnp.int32, (owners, owners), 1)
    turned = jnp.where(row == column, jnp.broadcast_to(counts_ref[...], (owners, owners)), 0)
    counts = jnp.sum(turned.astype(F32), axis=1, keepdims=True).astype(jnp.int32)
    slots = lax.broadcasted_iota(jnp.int32, (rows, LANES), 1)
    for n in range(chunks):
        first = n * rows
        for copy in in_copies[n]:
            copy.wait()
        for j in range(capacity // LANES):
            cols = slice(j * LANES, (j + 1) * LANES)
            out_ref[pl.ds(first * 8 + j, rows, stride=8), :] = positions_ref[first : first + rows, cols]
            live = slots + j * LANES < counts[first : first + rows]
            out_ref[pl.ds(first * 8 + 4 + j, rows, stride=8), :] = jnp.where(
                live, masses_ref[first : first + rows, cols].astype(F32), 0.0
            )
        for copy in out_copies[n]:
            copy.start()
    for copies in out_copies:
        for copy in copies:
            copy.wait()


def deposit_kernel(got_ref, acc_ref):
    sources = got_ref.shape[0]
    zero = jnp.zeros((), BF16)

    def deposit():
        row_id = row_ids(ROWS)
        sub_id = lax.broadcasted_iota(jnp.int32, (SUB, LANES), 0)
        lane_ids = [(TILES * sub_id + t).astype(F32).astype(BF16) for t in range(TILES)]
        highs, lows = [], []
        for s in range(sources):
            tile = got_ref[s]
            places, mass = tile[0:4], tile[4:8]
            floored = jnp.floor(places)
            fraction = places - floored
            pixel = floored.astype(jnp.int32) & (CYCLE_LEN - 1)
            high = (pixel >> 7).astype(F32)
            low = (pixel & (LANES - 1)).astype(F32)
            near = 1.0 - fraction
            for r in range(4):
                highs.append(
                    jnp.where(spread_row(high, r, ROWS) == row_id, spread_row(mass, r, ROWS), zero)
                )
                low_r, near_r, far_r = (spread_row(v, r, SUB) for v in (low, near, fraction))
                hits = [low_r == lane_id for lane_id in lane_ids]
                tiles = [jnp.where(hits[0], near_r, zero)]
                for t in range(1, TILES):
                    tiles.append(jnp.where(hits[t], near_r, jnp.where(hits[t - 1], far_r, zero)))
                tiles.append(jnp.where(hits[-1], far_r, zero))
                lows.append(jnp.concatenate(tiles, axis=0))
        return lax.dot_general(
            jnp.concatenate(highs, axis=1),
            jnp.concatenate(lows, axis=1),
            NT,
            preferred_element_type=F32,
        )

    acc_ref[:, LANES:] = jnp.zeros((ROWS, LANES), F32)
    acc_ref[:, :COLUMNS] = deposit()


def hits_kernel(order_ref, places_ref, out_ref, side_ref, block=None):
    if block is None:
        block = lax.axis_index(("x", "core", "z_hi", "z_lo", "y"))
    zero, one = jnp.zeros((), BF16), jnp.ones((), BF16)
    planes = order_ref.shape[0] // 8
    cycles = places_ref.shape[1]

    row = lax.broadcasted_iota(jnp.int32, (cycles, cycles), 0)
    column = lax.broadcasted_iota(jnp.int32, (cycles, cycles), 1)
    half = cycles // 2
    taken = jnp.where(row == 2 * (column % half) + column // half, 1.0, 0.0).astype(BF16)
    places = jnp.broadcast_to(places_ref[...], (16, cycles)).astype(F32).astype(BF16)
    places = lax.dot_general(places, taken, NN, preferred_element_type=F32)[:8].astype(jnp.int32)
    own = jnp.broadcast_to(order_ref[pl.ds(block // 4, 1), :], side_ref.shape)
    own = pltpu.roll(own, lax.rem(LANES + cycles - lax.rem(block, 4) * 32, LANES), 1)
    side_lane = lax.broadcasted_iota(jnp.int32, side_ref.shape, 1)
    side_ref[...] = jnp.where(side_lane < cycles, jnp.concatenate([places, places], axis=1), own)

    def step(k, carry):
        ids = row_ids(ROWS)
        lower = (order_ref[pl.ds(k, 8, stride=planes), :] & (ROWS - 1)).astype(F32)
        hits = [jnp.where(spread_row(lower, r, ROWS) == ids, one, zero) for r in range(8)]
        out_ref[k] = jnp.concatenate(hits, axis=1)
        return carry

    lax.fori_loop(0, planes, step, 0)


def spectrum_kernel(
    acc_ref, order_ref, hits_ref, one_h_ref, one_l_ref, cos_ref, sin_ref, two_h_ref, two_l_ref, out_ref
):
    beyond = acc_ref[:, LANES:]
    column = lax.broadcasted_iota(jnp.int32, (ROWS, LANES), 1)
    next_row = pltpu.roll(pltpu.roll(beyond, LANES - SUB + 1, 1), 1, 0)
    cycle = acc_ref[:, :LANES] + jnp.where(
        column == 0, next_row, jnp.where(column < SUB, pltpu.roll(beyond, 1, 1), 0.0)
    )

    def dot(a, b, dims):
        return lax.dot_general(a, b, dims, preferred_element_type=F32)

    cycle_h, cycle_l = split(cycle)
    both = dot(one_h_ref[...], jnp.concatenate([cycle_h, cycle_l], axis=1), NN)
    first = both[:, :LANES] + (both[:, LANES:] + dot(one_l_ref[...], cycle_h, NN))
    real, imag = first[:ROWS], first[ROWS:]
    cos, sin = cos_ref[...], sin_ref[...]
    twisted = jnp.concatenate([real * cos + imag * sin, imag * cos - real * sin], axis=1)
    twisted_h, twisted_l = split(twisted)
    spectrum = (
        dot(two_h_ref[...], twisted_l, NT)
        + dot(two_l_ref[...], twisted_h, NT)
        + dot(two_h_ref[...], twisted_h, NT)
    )
    spectrum = spectrum.astype(BF16)
    upper_ids = lax.broadcasted_iota(jnp.int32, (UPPER, LANES), 0)
    planes = out_ref.shape[0]
    for k in range(planes):
        upper = order_ref[pl.ds(k, 8, stride=planes), :] >> 8
        picked = dot(spectrum, hits_ref[k], NN)
        reals, imags = [], []
        for r in range(8):
            cols = slice(r * LANES, (r + 1) * LANES)
            mine = jnp.broadcast_to(upper[r : r + 1, :], (UPPER, LANES)) == upper_ids
            reals.append(jnp.sum(jnp.where(mine, picked[:UPPER, cols], 0.0), axis=0, keepdims=True))
            imags.append(jnp.sum(jnp.where(mine, picked[UPPER:, cols], 0.0), axis=0, keepdims=True))
        rows = reals[::2] + imags[::2] + reals[1::2] + imags[1::2]
        out_ref[(k - FIRST_ON_LINE // 2) % planes] = jnp.concatenate(rows, axis=0).astype(BF16)


def slab_sum_kernel(parts_ref, out_ref):
    z_count = parts_ref.shape[0]
    quarter = lax.broadcasted_iota(jnp.int32, (4, LANES), 1) // 32
    for z_lo in range(2):
        total = parts_ref[z_lo].astype(F32)
        for z in range(z_lo + 2, z_count, 2):
            total = total + parts_ref[z].astype(F32)
        for y in range(4):
            row = jnp.zeros((4, LANES), F32)
            for n in range(4):
                shift = (n - y) % 4 * 32
                values = pltpu.roll(total, shift, 1) if shift else total
                row = jnp.where(quarter == n, values[4 * n : 4 * n + 4], row)
            for x in range(4):
                chip = (4 * y + x - FIRST_IN_PLANE) % 16
                out_ref[pl.ds(2 * chip + z_lo, 1), :] = row[x : x + 1]


def product_kernel(got_ref, side_ref, legendre_ref, out_ref):
    modes, cycles, width = legendre_ref.shape
    rows = 2 * modes
    before = FIRST_IN_PLANE
    got = []
    for z_lo in range(2):
        got.append(got_ref[pl.ds(2 * (16 - before) + z_lo, before, stride=2), :])
        got.append(got_ref[pl.ds(z_lo, 16 - before, stride=2), :])
    got = jnp.concatenate(got, axis=0)
    turned = jnp.transpose(got)
    turned = jnp.concatenate([turned[:rows], turned[rows:]], axis=1).astype(BF16)
    place = lax.broadcasted_iota(jnp.int32, (cycles, cycles), 0) == jnp.broadcast_to(
        side_ref[:1, :cycles], (cycles, cycles)
    )
    sky = lax.dot_general(
        turned, jnp.where(place, 1.0, 0.0).astype(BF16), NT, preferred_element_type=F32
    )
    sky = jnp.concatenate([sky, sky], axis=1)
    lane = lax.broadcasted_iota(jnp.int32, (rows, 2 * cycles), 1)
    mode = lax.broadcasted_iota(jnp.int32, (rows, 2 * cycles), 0) & (modes - 1)
    owner = jnp.where(lane < cycles, 0, 1)
    blocks = [
        jnp.where(mode == owner + 2 * t, sky, 0.0).astype(BF16) for t in range(modes // 2)
    ]
    table = legendre_ref[...].reshape(modes * cycles, width)
    product = lax.dot_general(
        jnp.concatenate(blocks, axis=1), table, NN, preferred_element_type=F32
    )
    row_mode = lax.broadcasted_iota(jnp.int32, (rows, LANES), 0) & (modes - 1)
    column = lax.broadcasted_iota(jnp.int32, (rows, LANES), 1) - cycles
    order = jnp.sum(
        jnp.where(row_mode == column, jnp.broadcast_to(side_ref[:1, :], (rows, LANES)), 0).astype(F32),
        axis=1,
        keepdims=True,
    )
    degree = (LMAX - LW + 1 + lax.broadcasted_iota(jnp.int32, (rows, width), 1)).astype(F32)
    product = jnp.where(degree >= order, product, 0.0)
    out_ref[pl.ds(0, modes, stride=2), :] = product[:modes]
    out_ref[pl.ds(1, modes, stride=2), :] = product[modes:]


def kernel_call(kernel, out_shape, dtype=F32, scratch=(), limit=32, **options):
    return pl.pallas_call(
        kernel,
        out_shape=jax.ShapeDtypeStruct(out_shape, dtype) if dtype else out_shape,
        scratch_shapes=list(scratch),
        compiler_params=pltpu.CompilerParams(vmem_limit_bytes=limit * 1024 * 1024),
        **options,
    )


def pack_call(owners, capacity):
    return kernel_call(
        pack_kernel,
        (owners * 8, LANES),
        scratch=[
            pltpu.VMEM((owners, capacity), F32),
            pltpu.VMEM((owners, capacity), BF16),
            pltpu.VMEM((1, owners), jnp.int32),
            pltpu.VMEM((owners * 8, LANES), F32),
            pltpu.SemaphoreType.DMA((5, 4)),
        ],
        limit=60,
        in_specs=[pl.BlockSpec(memory_space=pl.ANY)] * 3,
        out_specs=pl.BlockSpec(memory_space=pl.ANY),
    )


def hits_call(planes, kernel=hits_kernel):
    outs = [
        jax.ShapeDtypeStruct((planes, ROWS, M // planes), BF16),
        jax.ShapeDtypeStruct((8, LANES), jnp.int32),
    ]
    cost = pl.CostEstimate(flops=0, transcendentals=0, bytes_accessed=2 * ROWS * M)
    return kernel_call(kernel, outs, None, limit=16, cost_estimate=cost)


def exchange(values, axes, first):
    count = lax.axis_size(axes)
    members = [(first + n) % count for n in range(count)]
    return lax.all_to_all(
        values, axes, split_axis=0, concat_axis=0, axis_index_groups=[members], tiled=True
    )


def local(positions, masses, send_counts, legendre, cycle_order, m_order):
    z = ("z_hi", "z_lo")
    cycles = cycle_order.shape[0]
    planes = lax.axis_size(z)
    capacity = positions.shape[-1]
    mode_count = legendre.shape[0]
    order_rows = m_order.reshape(M // LANES, LANES)
    packed = pack_call(cycles, capacity)(
        positions.reshape(cycles, capacity),
        masses.reshape(cycles, capacity),
        send_counts.reshape(1, cycles),
    )
    got = exchange(packed.reshape(cycles, 8, LANES), ("z_lo", "y", "x", "core"), FIRST_IN_BLOCK)
    hits, side = hits_call(planes)(order_rows, cycle_order.reshape(1, cycles))
    cycle = kernel_call(
        deposit_kernel,
        (ROWS, 2 * LANES),
        cost_estimate=pl.CostEstimate(
            flops=2 * cycles * capacity * ROWS * 2 * LANES, transcendentals=0, bytes_accessed=2**19
        ),
    )(got)
    parts = kernel_call(spectrum_kernel, (planes, 2 * M // planes // LANES, LANES), BF16)(
        cycle, order_rows, hits, *tables()
    )
    parts = parts.reshape(2 * planes, M // planes // LANES, LANES)
    got_parts = exchange(parts, z + ("core",), FIRST_ON_LINE)
    own = kernel_call(slab_sum_kernel, (cycles // 2, LANES), limit=4)(
        got_parts.reshape(planes, 2 * M // planes // LANES, LANES)
    )
    spread = exchange(own.reshape(cycles // 4, 2, LANES), ("y", "x"), FIRST_IN_PLANE)
    alm = kernel_call(product_kernel, (2 * mode_count, LW), limit=8)(
        spread.reshape(cycles // 2, LANES), side, legendre
    )
    return alm.reshape(mode_count, 2, LW)


def solution(mesh):
    cut = jax.sharding.Mesh(
        mesh.devices.reshape(8, 2, 4, 4, 2), ("z_hi", "z_lo", "y", "x", "core")
    )
    blk, pslab = ("z_hi", "z_lo", "y"), ("x", "core")
    placed = (
        P(blk, pslab, None, None),
        P(blk, pslab, None, None),
        P(blk, pslab, None),
        P(pslab + blk, None, None),
        P(),
        P(),
    )
    return jax.shard_map(
        local,
        mesh=cut,
        in_specs=placed,
        out_specs=P(pslab + blk, None, None),
        check_vma=False,
    )
```

profile of v0, /device:TPU:1, one launch (start us, length us, event | category | flops | bytes accessed | tf_op | source)
XLA Modules:
  0.0 60.5 jit_solution(3127885739037590074)
XLA Ops:
  0.0 0.0 copy-start.4
  0.0 0.0 copy-start.5
  0.0 0.0 copy-start.6
  0.0 0.0 copy-start.7
  0.0 0.0 copy-start.8
  0.0 0.0 copy-start.9
  0.0 0.0 copy-start.10
  0.1 1.8 %shard_map.118 = f32[512,128]{1,0:T(8,128)} custom-call(f32[64,512]{1,0:T(8,128)} %bitcast.19, bf16[64,512]{1,0:T(8,128)(2,1)} %bitcast.20, s32[1,64]{1,0:T(1,128)} %bitcast.21), custom_call_target="tpu_custom_call" | custom-call | tf_op jit(solution)/shard_map/pallas_call | solution.py:353
  1.8 13.0 %all-to-all-start = ((f32[64,8,128]{2,1,0:T(8,128)}), f32[64,8,128]{2,1,0:T(8,128)S(1)}, u32[]{:S(2)}, u32[]{:S(2)}) async-start(f32[64,8,128]{2,1,0:T(8,128)} %bitcast.18), calls=%async_computation | async-start | bytes 524288 | tf_op jit(solution)/shard_map/all_to_all | solution.py:341
  14.8 0.0 copy-start.3
  14.8 0.8 %copy-done.3 = s32[16384]{0:T(1024)S(1)} copy-done((s32[16384]{0:T(1024)S(1)}, s32[16384]{0:T(1024)}, u32[]{:S(2)}) %copy-start.3) | copy-done | bytes 65560
  15.7 0.0 copy-start.11
  15.7 0.7 %copy-done.11 = s32[64]{0:T(128)S(1)} copy-done((s32[64]{0:T(128)S(1)}, s32[64]{0:T(128)}, u32[]{:S(2)}) %copy-start.11) | copy-done | bytes 280
  16.3 1.2 %shard_map.120 = (bf16[16,256,1024]{2,1,0:T(8,128)(2,1)S(1)}, s32[8,128]{1,0:T(8,128)S(1)}) custom-call(s32[128,128]{1,0:T(8,128)S(1)} %bitcast.11, s32[1,64]{1,0:T(1,128)S(1)} %bitcast.17), custom_call_target="tpu_custom_call" | custom-call | bytes 8388608 | tf_op jit(solution)/shard_map/pallas_call | solution.py:359
  17.6 0.0 copy-start
  17.6 3.2 %copy-done = bf16[16,256,1024]{2,1,0:T(8,128)(2,1)} copy-done((bf16[16,256,1024]{2,1,0:T(8,128)(2,1)}, bf16[16,256,1024]{2,1,0:T(8,128)(2,1)S(1)}, u32[]{:S(2)}) %copy-start) | copy-done | bytes 8388632
  20.8 0.4 all-to-all-done.got_ref
  21.2 0.0 copy-start.1
  21.2 4.5 %shard_map.119.acc_ref = f32[256,256]{1,0:T(8,128)S(1)} custom-call(f32[64,8,128]{2,1,0:T(8,128)S(1)} %all-to-all-done.got_ref), custom_call_target="tpu_custom_call" | custom-call | flops 4294967296 | bytes 524288 | tf_op jit(solution)/shard_map/pallas_call | solution.py:360
  25.7 0.0 copy-start.2
  25.7 0.0 copy-done.4
  25.8 0.0 copy-done.5
  25.8 0.0 copy-done.6
  25.8 0.0 copy-done.7
  25.8 0.0 copy-done.8
  25.8 0.0 copy-done.9
  25.8 0.0 copy-done.10
  25.8 0.0 copy-done.1
  25.8 2.4 %shard_map.121 = bf16[16,16,128]{2,1,0:T(8,128)(2,1)S(1)} custom-call(f32[256,256]{1,0:T(8,128)S(1)} %shard_map.119.acc_ref, s32[128,128]{1,0:T(8,128)S(1)} %bitcast.12, bf16[16,256,1024]{2,1,0:T(8,128)(2,1)S(1)} %copy-done.1, bf16[512,256]{1,0:T(8,128)(2,1)S(1)} %copy-done.6, bf16[512,256]{1,0:T(8,128)(2,1)S(1)} %copy-done.5, f32[256,128]{1,0:T(8,128)S(1)} %copy-done.8, ...), custom_call_target="tpu_custom_call" | custom-call | tf_op jit(solution)/shard_map/pallas_call | solution.py:367
  28.2 20.6 %all_to_all.15 = bf16[32,8,128]{2,1,0:T(8,128)(2,1)S(1)} all-to-all(bf16[32,8,128]{2,1,0:T(8,128)(2,1)S(1)} %bitcast.13), channel_id=1, replica_groups={{256,257,288,289,320,321,352,353,384,385,416,417,448,449,480,481,0,1,32..., dimensions={0} | all-to-all | bytes 131072 | tf_op jit(solution)/shard_map/all_to_all | solution.py:341
  48.8 0.1 shard_map.122
  48.9 10.4 %all_to_all.16 = f32[16,2,128]{2,1,0:T(2,128)S(1)} all-to-all(f32[16,2,128]{2,1,0:T(2,128)S(1)} %bitcast.16), channel_id=1, replica_groups={{18,20,22,24,26,28,30,0,2,4,6,8,10,12,14,16},{19,21,23,25,27,29,31,1,3,..., dimensions={0} | all-to-all | bytes 32768 | tf_op jit(solution)/shard_map/all_to_all | solution.py:341
  59.3 0.0 copy-done.2
  59.3 1.2 %shard_map.123 = f32[64,128]{1,0:T(8,128)} custom-call(f32[32,128]{1,0:T(8,128)S(1)} %bitcast.15, s32[8,128]{1,0:T(8,128)S(1)} %get-tuple-element.8.side_ref, bf16[32,64,128]{2,1,0:T(8,128)(2,1)S(1)} %copy-done.2), custom_call_target="tpu_custom_call" | custom-call | tf_op jit(solution)/shard_map/pallas_call | solution.py:376
Async XLA Ops:
  0.0 25.7 %copy-start.4 = (s32[16384]{0:T(1024)S(1)}, s32[16384]{0:T(1024)}, u32[]{:S(2)}) copy-start(s32[16384]{0:T(1024)} %param.17) | copy-start | bytes 196612
  0.0 25.8 %copy-start.5 = (bf16[512,256]{1,0:T(8,128)(2,1)S(1)}, bf16[512,256]{1,0:T(8,128)(2,1)}, u32[]{:S(2)}) copy-start(bf16[512,256]{1,0:T(8,128)(2,1)} %constant.13.clone.one_l_ref) | copy-start | bytes 786436
  0.0 25.8 %copy-start.6 = (bf16[512,256]{1,0:T(8,128)(2,1)S(1)}, bf16[512,256]{1,0:T(8,128)(2,1)}, u32[]{:S(2)}) copy-start(bf16[512,256]{1,0:T(8,128)(2,1)} %constant.12.clone.one_h_ref) | copy-start | bytes 786436
  0.0 25.8 %copy-start.7 = (f32[256,128]{1,0:T(8,128)S(1)}, f32[256,128]{1,0:T(8,128)}, u32[]{:S(2)}) copy-start(f32[256,128]{1,0:T(8,128)} %constant.15.clone.sin_ref) | copy-start | bytes 393220
  0.0 25.8 %copy-start.8 = (f32[256,128]{1,0:T(8,128)S(1)}, f32[256,128]{1,0:T(8,128)}, u32[]{:S(2)}) copy-start(f32[256,128]{1,0:T(8,128)} %constant.14.clone.cos_ref) | copy-start | bytes 393220
  0.0 25.8 %copy-start.9 = (bf16[128,256]{1,0:T(8,128)(2,1)S(1)}, bf16[128,256]{1,0:T(8,128)(2,1)}, u32[]{:S(2)}) copy-start(bf16[128,256]{1,0:T(8,128)(2,1)} %constant.17.clone.two_l_ref) | copy-start | bytes 196612
  0.0 25.8 %copy-start.10 = (bf16[128,256]{1,0:T(8,128)(2,1)S(1)}, bf16[128,256]{1,0:T(8,128)(2,1)}, u32[]{:S(2)}) copy-start(bf16[128,256]{1,0:T(8,128)(2,1)} %constant.16.clone.two_h_ref) | copy-start | bytes 196612
  1.8 19.4 %all-to-all-start = ((f32[64,8,128]{2,1,0:T(8,128)}), f32[64,8,128]{2,1,0:T(8,128)S(1)}, u32[]{:S(2)}, u32[]{:S(2)}) async-start(f32[64,8,128]{2,1,0:T(8,128)} %bitcast.18), calls=%async_computation | async-start | bytes 524288 | tf_op jit(solution)/shard_map/all_to_all | solution.py:341
  14.8 0.8 %copy-start.3 = (s32[16384]{0:T(1024)S(1)}, s32[16384]{0:T(1024)}, u32[]{:S(2)}) copy-start(s32[16384]{0:T(1024)} %param.17) | copy-start | bytes 196612
  15.7 0.7 %copy-start.11 = (s32[64]{0:T(128)S(1)}, s32[64]{0:T(128)}, u32[]{:S(2)}) copy-start(s32[64]{0:T(128)} %param.16) | copy-start | bytes 772
  17.6 3.2 %copy-start = (bf16[16,256,1024]{2,1,0:T(8,128)(2,1)}, bf16[16,256,1024]{2,1,0:T(8,128)(2,1)S(1)}, u32[]{:S(2)}) copy-start(bf16[16,256,1024]{2,1,0:T(8,128)(2,1)S(1)} %get-tuple-element.7.hits_ref) | copy-start | bytes 25165828
  21.2 4.6 %copy-start.1 = (bf16[16,256,1024]{2,1,0:T(8,128)(2,1)S(1)}, bf16[16,256,1024]{2,1,0:T(8,128)(2,1)}, u32[]{:S(2)}) copy-start(bf16[16,256,1024]{2,1,0:T(8,128)(2,1)} %copy-done) | copy-start | bytes 25165828
  25.7 33.6 %copy-start.2 = (bf16[32,64,128]{2,1,0:T(8,128)(2,1)S(1)}, bf16[32,64,128]{2,1,0:T(8,128)(2,1)}, u32[]{:S(2)}) copy-start(bf16[32,64,128]{2,1,0:T(8,128)(2,1)} %legendre_ref.1) | copy-start | bytes 1572868
where the time goes:
time: 60.8 us; the launch traced here: 60.5 us
  blocking collectives  31 us (51%)
  starting transfers between devices  13 us (21%)
  Pallas kernels  11.2 us (18%)
  local copies, waits for them, and re-layouts  4.75 us (8%)
    all_to_all x2, blocking collectives, exchange(): lax.all_to_all(values, axes, split_axis=0, concat_axis=0, axis_index_grou...  31 us
    all_to_all x1, starting transfers between devices, exchange(): lax.all_to_all(values, axes, split_axis=0, concat_axis=0, axis_index_grou...  13 us
    unnamed x24, local copies, waits for them, and re-layouts  4.75 us
    pallas_call x1, Pallas kernels, local(): kernel_call(deposit_kernel, (ROWS, 2 * LANES), cost_estimate=pl.CostEstim...  4.5 us
    pallas_call x1, Pallas kernels, local(): kernel_call(spectrum_kernel, (planes, 2 * M // planes // LANES, LANES), B...  2.41 us
    pallas_call x1, Pallas kernels, local(): pack_call(cycles, capacity)  1.76 us
    pallas_call x1, Pallas kernels, local(): hits, side = hits_call(planes)(order_rows, cycle_order.reshape(1, cycles))  1.25 us
  transfers between devices with their start and end apart: 1, of which 1 were waited for; matrix products, arithmetic and copies ran while one was open for 0% of the time, Pallas kernels for 2%

commit v1 on v0

--- a/solution.py
+++ b/solution.py
@@ -20,9 +20,9 @@
 SUB = LANES // TILES
 COLUMNS = (TILES + 1) * SUB
 
-FIRST_IN_BLOCK = 18
+FIRST_IN_BLOCK = 20
 FIRST_ON_LINE = 16
-FIRST_IN_PLANE = 9
+FIRST_IN_PLANE = 10
 
 F32 = jnp.float32
 BF16 = jnp.bfloat16
@@ -171,12 +171,31 @@
     acc_ref[:, :COLUMNS] = deposit()
 
 
-def hits_kernel(order_ref, places_ref, out_ref, side_ref, block=None):
+def hits_kernel(
+    order_hbm, places_hbm, out_hbm, side_hbm, order_ref, places_ref, out_ref, side_ref, sems, block=None
+):
     if block is None:
         block = lax.axis_index(("x", "core", "z_hi", "z_lo", "y"))
     zero, one = jnp.zeros((), BF16), jnp.ones((), BF16)
     planes = order_ref.shape[0] // 8
     cycles = places_ref.shape[1]
+    order_copy = pltpu.make_async_copy(order_hbm, order_ref, sems.at[planes])
+    places_copy = pltpu.make_async_copy(places_hbm, places_ref, sems.at[planes + 1])
+    side_copy = pltpu.make_async_copy(side_ref, side_hbm, sems.at[planes + 2])
+    out_copies = [
+        pltpu.make_async_copy(out_ref.at[k], out_hbm.at[k], sems.at[k]) for k in range(planes)
+    ]
+    order_copy.start()
+    places_copy.start()
+    order_copy.wait()
+    places_copy.wait()
+
+    ids = row_ids(ROWS)
+    for k in range(planes):
+        lower = (order_ref[pl.ds(k, 8, stride=planes), :] & (ROWS - 1)).astype(F32)
+        hits = [jnp.where(spread_row(lower, r, ROWS) == ids, one, zero) for r in range(8)]
+        out_ref[k] = jnp.concatenate(hits, axis=1)
+        out_copies[k].start()
 
     row = lax.broadcasted_iota(jnp.int32, (cycles, cycles), 0)
     column = lax.broadcasted_iota(jnp.int32, (cycles, cycles), 1)
@@ -188,15 +207,10 @@
     own = pltpu.roll(own, lax.rem(LANES + cycles - lax.rem(block, 4) * 32, LANES), 1)
     side_lane = lax.broadcasted_iota(jnp.int32, side_ref.shape, 1)
     side_ref[...] = jnp.where(side_lane < cycles, jnp.concatenate([places, places], axis=1), own)
-
-    def step(k, carry):
-        ids = row_ids(ROWS)
-        lower = (order_ref[pl.ds(k, 8, stride=planes), :] & (ROWS - 1)).astype(F32)
-        hits = [jnp.where(spread_row(lower, r, ROWS) == ids, one, zero) for r in range(8)]
-        out_ref[k] = jnp.concatenate(hits, axis=1)
-        return carry
-
-    lax.fori_loop(0, planes, step, 0)
+    side_copy.start()
+    for copy in out_copies:
+        copy.wait()
+    side_copy.wait()
 
 
 def spectrum_kernel(
@@ -332,7 +346,22 @@
         jax.ShapeDtypeStruct((8, LANES), jnp.int32),
     ]
     cost = pl.CostEstimate(flops=0, transcendentals=0, bytes_accessed=2 * ROWS * M)
-    return kernel_call(kernel, outs, None, limit=16, cost_estimate=cost)
+    return kernel_call(
+        kernel,
+        outs,
+        None,
+        scratch=[
+            pltpu.VMEM((M // LANES, LANES), jnp.int32),
+            pltpu.VMEM((1, 64), jnp.int32),
+            pltpu.VMEM((planes, ROWS, M // planes), BF16),
+            pltpu.VMEM((8, LANES), jnp.int32),
+            pltpu.SemaphoreType.DMA((planes + 3,)),
+        ],
+        limit=60,
+        cost_estimate=cost,
+        in_specs=[pl.BlockSpec(memory_space=pl.ANY)] * 2,
+        out_specs=[pl.BlockSpec(memory_space=pl.ANY)] * 2,
+    )
 
 
 def exchange(values, axes, first):

time: 60.8 us -> 58.3 us (0.959)
  local copies, waits for them, and re-layouts: 4.75 us -> 0.05 us
  Pallas kernels: 11.2 us -> 14.4 us
  blocking collectives: 31 us -> 28.7 us
  starting transfers between devices: 13 us -> 14.5 us
    unnamed x24 -> x20, local copies, waits for them, and re-layouts: 4.75 us -> 0.05 us
    pallas_call x1, Pallas kernels: 1.25 us -> 4.37 us  [local(): hits, side = hits_call(planes)(order_rows, cycle_order.reshape(1, cycles))]
    all_to_all x2, blocking collectives: 31 us -> 28.7 us  [exchange(): lax.all_to_all(values, axes, split_axis=0, concat_axis=0, axis_index_grou...]
    all_to_all x1, starting transfers between devices: 13 us -> 14.5 us  [exchange(): lax.all_to_all(values, axes, split_axis=0, concat_axis=0, axis_index_grou...]
  transfers between devices with their start and end apart: 1 -> 1, of which waited for: 1 -> 1; matrix products, arithmetic and copies ran while one was open for 0% -> 0% of each run, Pallas kernels for 2% -> 8%
where the time goes in v1:
time: 58.3 us; the launch traced here: 58.1 us
  blocking collectives  28.7 us (49%)
  starting transfers between devices  14.5 us (25%)
  Pallas kernels  14.4 us (25%)
    all_to_all x2, blocking collectives, exchange(): lax.all_to_all(values, axes, split_axis=0, concat_axis=0, axis_index_grou...  28.7 us
    all_to_all x1, starting transfers between devices, exchange(): lax.all_to_all(values, axes, split_axis=0, concat_axis=0, axis_index_grou...  14.5 us
    pallas_call x1, Pallas kernels, local(): kernel_call(deposit_kernel, (ROWS, 2 * LANES), cost_estimate=pl.CostEstim...  4.5 us
    pallas_call x1, Pallas kernels, local(): hits, side = hits_call(planes)(order_rows, cycle_order.reshape(1, cycles))  4.37 us
    pallas_call x1, Pallas kernels, local(): kernel_call(spectrum_kernel, (planes, 2 * M // planes // LANES, LANES), B...  2.48 us
    pallas_call x1, Pallas kernels, local(): pack_call(cycles, capacity)  1.77 us
    pallas_call x1, Pallas kernels, local(): kernel_call(product_kernel, (2 * mode_count, LW), limit=8)  1.17 us
  transfers between devices with their start and end apart: 1, of which 1 were waited for; matrix products, arithmetic and copies ran while one was open for 0% of the time, Pallas kernels for 8%

profile of v1, /device:TPU:1, one launch (start us, length us, event | category | flops | bytes accessed | tf_op | source)
XLA Modules:
  0.0 58.1 jit_solution(44474651710660901)
XLA Ops:
  0.0 0.0 copy-start.2
  0.0 0.0 copy-start.3
  0.0 0.0 copy-start.4
  0.0 0.0 copy-start.5
  0.0 0.0 copy-start.6
  0.0 0.0 copy-start.7
  0.0 0.0 copy-start.8
  0.1 1.8 %shard_map.118 = f32[512,128]{1,0:T(8,128)} custom-call(f32[64,512]{1,0:T(8,128)} %bitcast.18, bf16[64,512]{1,0:T(8,128)(2,1)} %bitcast.19, s32[1,64]{1,0:T(1,128)} %bitcast.21), custom_call_target="tpu_custom_call" | custom-call | tf_op jit(solution)/shard_map/pallas_call | solution.py:382
  1.8 14.5 %all-to-all-start = ((f32[64,8,128]{2,1,0:T(8,128)}), f32[64,8,128]{2,1,0:T(8,128)S(1)}, u32[]{:S(2)}, u32[]{:S(2)}) async-start(f32[64,8,128]{2,1,0:T(8,128)} %bitcast.17), calls=%async_computation | async-start | bytes 524288 | tf_op jit(solution)/shard_map/all_to_all | solution.py:370
  16.3 4.4 %shard_map.120 = (bf16[16,256,1024]{2,1,0:T(8,128)(2,1)}, s32[8,128]{1,0:T(8,128)}) custom-call(s32[128,128]{1,0:T(8,128)} %bitcast.11, s32[1,64]{1,0:T(1,128)} %bitcast.20), custom_call_target="tpu_custom_call" | custom-call | bytes 8388608 | tf_op jit(solution)/shard_map/pallas_call | solution.py:388
  20.7 0.3 all-to-all-done.got_ref
  21.0 0.0 copy-start
  21.0 4.5 %shard_map.119.acc_ref = f32[256,256]{1,0:T(8,128)S(1)} custom-call(f32[64,8,128]{2,1,0:T(8,128)S(1)} %all-to-all-done.got_ref), custom_call_target="tpu_custom_call" | custom-call | flops 4294967296 | bytes 524288 | tf_op jit(solution)/shard_map/pallas_call | solution.py:389
  25.5 0.0 copy-start.1
  25.5 0.0 copy-start.9
  25.5 0.0 copy-done.2
  25.5 0.0 copy-done.3
  25.6 0.0 copy-done.4
  25.6 0.0 copy-done.5
  25.6 0.0 copy-done.6
  25.6 0.0 copy-done.7
  25.6 0.0 copy-done.8
  25.6 0.0 copy-done
  25.6 2.5 %shard_map.121 = bf16[16,16,128]{2,1,0:T(8,128)(2,1)S(1)} custom-call(f32[256,256]{1,0:T(8,128)S(1)} %shard_map.119.acc_ref, s32[128,128]{1,0:T(8,128)S(1)} %bitcast.12, bf16[16,256,1024]{2,1,0:T(8,128)(2,1)S(1)} %copy-done, bf16[512,256]{1,0:T(8,128)(2,1)S(1)} %copy-done.4, bf16[512,256]{1,0:T(8,128)(2,1)S(1)} %copy-done.3, f32[256,128]{1,0:T(8,128)S(1)} %copy-done.6, ...), custom_call_target="tpu_custom_call" | custom-call | tf_op jit(solution)/shard_map/pallas_call | solution.py:396
  28.1 19.8 %all_to_all.15 = bf16[32,8,128]{2,1,0:T(8,128)(2,1)S(1)} all-to-all(bf16[32,8,128]{2,1,0:T(8,128)(2,1)S(1)} %bitcast.13), channel_id=1, replica_groups={{256,257,288,289,320,321,352,353,384,385,416,417,448,449,480,481,0,1,32..., dimensions={0} | all-to-all | bytes 131072 | tf_op jit(solution)/shard_map/all_to_all | solution.py:370
  47.9 0.1 shard_map.122
  48.0 8.8 %all_to_all.16 = f32[16,2,128]{2,1,0:T(2,128)S(1)} all-to-all(f32[16,2,128]{2,1,0:T(2,128)S(1)} %bitcast.16), channel_id=1, replica_groups={{20,22,24,26,28,30,0,2,4,6,8,10,12,14,16,18},{21,23,25,27,29,31,1,3,5,7..., dimensions={0} | all-to-all | bytes 32768 | tf_op jit(solution)/shard_map/all_to_all | solution.py:370
  56.9 0.0 copy-done.1
  56.9 0.0 copy-done.9
  56.9 1.2 %shard_map.123 = f32[64,128]{1,0:T(8,128)} custom-call(f32[32,128]{1,0:T(8,128)S(1)} %bitcast.15, s32[8,128]{1,0:T(8,128)S(1)} %copy-done.9, bf16[32,64,128]{2,1,0:T(8,128)(2,1)S(1)} %copy-done.1), custom_call_target="tpu_custom_call" | custom-call | tf_op jit(solution)/shard_map/pallas_call | solution.py:405
Async XLA Ops:
  0.0 25.5 %copy-start.2 = (s32[16384]{0:T(1024)S(1)}, s32[16384]{0:T(1024)}, u32[]{:S(2)}) copy-start(s32[16384]{0:T(1024)} %param.17) | copy-start | bytes 196612
  0.0 25.5 %copy-start.3 = (bf16[512,256]{1,0:T(8,128)(2,1)S(1)}, bf16[512,256]{1,0:T(8,128)(2,1)}, u32[]{:S(2)}) copy-start(bf16[512,256]{1,0:T(8,128)(2,1)} %constant.13.clone.one_l_ref) | copy-start | bytes 786436
  0.0 25.6 %copy-start.4 = (bf16[512,256]{1,0:T(8,128)(2,1)S(1)}, bf16[512,256]{1,0:T(8,128)(2,1)}, u32[]{:S(2)}) copy-start(bf16[512,256]{1,0:T(8,128)(2,1)} %constant.12.clone.one_h_ref) | copy-start | bytes 786436
  0.0 25.6 %copy-start.5 = (f32[256,128]{1,0:T(8,128)S(1)}, f32[256,128]{1,0:T(8,128)}, u32[]{:S(2)}) copy-start(f32[256,128]{1,0:T(8,128)} %constant.15.clone.sin_ref) | copy-start | bytes 393220
  0.0 25.6 %copy-start.6 = (f32[256,128]{1,0:T(8,128)S(1)}, f32[256,128]{1,0:T(8,128)}, u32[]{:S(2)}) copy-start(f32[256,128]{1,0:T(8,128)} %constant.14.clone.cos_ref) | copy-start | bytes 393220
  0.0 25.6 %copy-start.7 = (bf16[128,256]{1,0:T(8,128)(2,1)S(1)}, bf16[128,256]{1,0:T(8,128)(2,1)}, u32[]{:S(2)}) copy-start(bf16[128,256]{1,0:T(8,128)(2,1)} %constant.17.clone.two_l_ref) | copy-start | bytes 196612
  0.0 25.5 %copy-start.8 = (bf16[128,256]{1,0:T(8,128)(2,1)S(1)}, bf16[128,256]{1,0:T(8,128)(2,1)}, u32[]{:S(2)}) copy-start(bf16[128,256]{1,0:T(8,128)(2,1)} %constant.16.clone.two_h_ref) | copy-start | bytes 196612
  1.8 19.2 %all-to-all-start = ((f32[64,8,128]{2,1,0:T(8,128)}), f32[64,8,128]{2,1,0:T(8,128)S(1)}, u32[]{:S(2)}, u32[]{:S(2)}) async-start(f32[64,8,128]{2,1,0:T(8,128)} %bitcast.17), calls=%async_computation | async-start | bytes 524288 | tf_op jit(solution)/shard_map/all_to_all | solution.py:370
  21.0 4.6 %copy-start = (bf16[16,256,1024]{2,1,0:T(8,128)(2,1)S(1)}, bf16[16,256,1024]{2,1,0:T(8,128)(2,1)}, u32[]{:S(2)}) copy-start(bf16[16,256,1024]{2,1,0:T(8,128)(2,1)} %get-tuple-element.7.hits_ref) | copy-start | bytes 25165828
  25.5 31.4 %copy-start.1 = (bf16[32,64,128]{2,1,0:T(8,128)(2,1)S(1)}, bf16[32,64,128]{2,1,0:T(8,128)(2,1)}, u32[]{:S(2)}) copy-start(bf16[32,64,128]{2,1,0:T(8,128)(2,1)} %legendre_ref.1) | copy-start | bytes 1572868
  25.5 31.4 %copy-start.9 = (s32[8,128]{1,0:T(8,128)S(1)}, s32[8,128]{1,0:T(8,128)}, u32[]{:S(2)}) copy-start(s32[8,128]{1,0:T(8,128)} %get-tuple-element.8.side_ref) | copy-start | bytes 12292

commit v2 on v1

--- a/solution.py
+++ b/solution.py
@@ -78,34 +78,23 @@
     return lax.broadcasted_iota(jnp.int32, (count, LANES), 0).astype(F32).astype(BF16)
 
 
-def pack_kernel(positions_hbm, masses_hbm, counts_hbm, out_hbm, positions_ref, masses_ref, counts_ref, out_ref, sems):
+def pack_kernel(positions_hbm, masses_hbm, counts_hbm, out_ref, positions_ref, masses_ref, counts_ref, sems):
     owners, capacity = positions_ref.shape
     rows = 16
     chunks = owners // rows
-    in_copies, out_copies = [], []
+    copies = []
     for n in range(chunks):
         part = pl.ds(n * rows, rows)
-        in_copies.append(
+        copies.append(
             (
                 pltpu.make_async_copy(positions_hbm.at[part, :], positions_ref.at[part, :], sems.at[n, 0]),
                 pltpu.make_async_copy(masses_hbm.at[part, :], masses_ref.at[part, :], sems.at[n, 1]),
             )
         )
-        cuts = sorted({n * rows, min(max(FIRST_IN_BLOCK, n * rows), (n + 1) * rows), (n + 1) * rows})
-        out_copies.append(
-            [
-                pltpu.make_async_copy(
-                    out_ref.at[pl.ds(8 * a, 8 * (b - a)), :],
-                    out_hbm.at[pl.ds(8 * ((a - FIRST_IN_BLOCK) % owners), 8 * (b - a)), :],
-                    sems.at[n, 2 + m],
-                )
-                for m, (a, b) in enumerate(zip(cuts, cuts[1:]))
-            ]
-        )
     counts_copy = pltpu.make_async_copy(counts_hbm, counts_ref, sems.at[chunks, 0])
     counts_copy.start()
-    for copies in in_copies:
-        for copy in copies:
+    for pair in copies:
+        for copy in pair:
             copy.start()
     counts_copy.wait()
     row = lax.broadcasted_iota(jnp.int32, (owners, owners), 0)
@@ -115,20 +104,19 @@
     slots = lax.broadcasted_iota(jnp.int32, (rows, LANES), 1)
     for n in range(chunks):
         first = n * rows
-        for copy in in_copies[n]:
+        cut = min(max(FIRST_IN_BLOCK - first, 0), rows)
+        pieces = [(a, b) for a, b in ((0, cut), (cut, rows)) if b > a]
+        for copy in copies[n]:
             copy.wait()
         for j in range(capacity // LANES):
             cols = slice(j * LANES, (j + 1) * LANES)
-            out_ref[pl.ds(first * 8 + j, rows, stride=8), :] = positions_ref[first : first + rows, cols]
+            places = positions_ref[first : first + rows, cols]
             live = slots + j * LANES < counts[first : first + rows]
-            out_ref[pl.ds(first * 8 + 4 + j, rows, stride=8), :] = jnp.where(
-                live, masses_ref[first : first + rows, cols].astype(F32), 0.0
-            )
-        for copy in out_copies[n]:
-            copy.start()
-    for copies in out_copies:
-        for copy in copies:
-            copy.wait()
+            weights = jnp.where(live, masses_ref[first : first + rows, cols].astype(F32), 0.0)
+            for a, b in pieces:
+                base = 8 * ((first + a - FIRST_IN_BLOCK) % owners)
+                out_ref[pl.ds(base + j, b - a, stride=8), :] = places[a:b]
+                out_ref[pl.ds(base + 4 + j, b - a, stride=8), :] = weights[a:b]
 
 
 def deposit_kernel(got_ref, acc_ref):
@@ -331,12 +319,10 @@
             pltpu.VMEM((owners, capacity), F32),
             pltpu.VMEM((owners, capacity), BF16),
             pltpu.VMEM((1, owners), jnp.int32),
-            pltpu.VMEM((owners * 8, LANES), F32),
-            pltpu.SemaphoreType.DMA((5, 4)),
+            pltpu.SemaphoreType.DMA((5, 2)),
         ],
-        limit=60,
+        limit=4,
         in_specs=[pl.BlockSpec(memory_space=pl.ANY)] * 3,
-        out_specs=pl.BlockSpec(memory_space=pl.ANY),
     )
 
 
@@ -379,10 +365,13 @@
     capacity = positions.shape[-1]
     mode_count = legendre.shape[0]
     order_rows = m_order.reshape(M // LANES, LANES)
-    packed = pack_call(cycles, capacity)(
+    particles = (
         positions.reshape(cycles, capacity),
         masses.reshape(cycles, capacity),
         send_counts.reshape(1, cycles),
+    )
+    packed = pack_call(cycles, capacity)(
+        *(pltpu.with_memory_space_constraint(value, pltpu.HBM) for value in particles)
     )
     got = exchange(packed.reshape(cycles, 8, LANES), ("z_lo", "y", "x", "core"), FIRST_IN_BLOCK)
     hits, side = hits_call(planes)(order_rows, cycle_order.reshape(1, cycles))

time: 58.3 us -> 58.2 us (level)
  no operation moved by 1% of the time
where the time goes in v2:
time: 58.2 us; the launch traced here: 57.9 us
  blocking collectives  28.7 us (49%)
  starting transfers between devices  14.5 us (25%)
  Pallas kernels  14.3 us (25%)
    all_to_all x2, blocking collectives, exchange(): lax.all_to_all(values, axes, split_axis=0, concat_axis=0, axis_index_grou...  28.7 us
    all_to_all x1, starting transfers between devices, exchange(): lax.all_to_all(values, axes, split_axis=0, concat_axis=0, axis_index_grou...  14.5 us
    pallas_call x1, Pallas kernels, local(): kernel_call(deposit_kernel, (ROWS, 2 * LANES), cost_estimate=pl.CostEstim...  4.5 us
    pallas_call x1, Pallas kernels, local(): hits, side = hits_call(planes)(order_rows, cycle_order.reshape(1, cycles))  4.37 us
    pallas_call x1, Pallas kernels, local(): kernel_call(spectrum_kernel, (planes, 2 * M // planes // LANES, LANES), B...  2.4 us
    pallas_call x1, Pallas kernels, local(): pack_call(cycles, capacity)  1.74 us
    pallas_call x1, Pallas kernels, local(): kernel_call(product_kernel, (2 * mode_count, LW), limit=8)  1.17 us
  transfers between devices with their start and end apart: 1, of which 1 were waited for; matrix products, arithmetic and copies ran while one was open for 0% of the time, Pallas kernels for 8%

profile of v2, /device:TPU:1, one launch (start us, length us, event | category | flops | bytes accessed | tf_op | source)
XLA Modules:
  0.0 57.9 jit_solution(12771670593339556715)
XLA Ops:
  0.0 0.0 copy-start.2
  0.0 0.0 copy-start.3
  0.0 0.0 copy-start.4
  0.0 0.0 copy-start.5
  0.0 0.0 copy-start.6
  0.0 0.0 copy-start.7
  0.0 0.0 copy-start.8
  0.1 1.7 %shard_map.118 = f32[512,128]{1,0:T(8,128)} custom-call(f32[64,512]{1,0:T(8,128)} %bitcast.17, bf16[64,512]{1,0:T(8,128)(2,1)} %bitcast.18, s32[1,64]{1,0:T(1,128)} %bitcast.20), custom_call_target="tpu_custom_call" | custom-call | tf_op jit(solution)/shard_map/pallas_call | solution.py:373
  1.8 14.5 %all-to-all-start = ((f32[64,8,128]{2,1,0:T(8,128)}), f32[64,8,128]{2,1,0:T(8,128)S(1)}, u32[]{:S(2)}, u32[]{:S(2)}) async-start(f32[64,8,128]{2,1,0:T(8,128)} %bitcast.3), calls=%async_computation | async-start | bytes 524288 | tf_op jit(solution)/shard_map/all_to_all | solution.py:356
  16.3 4.4 %shard_map.120 = (bf16[16,256,1024]{2,1,0:T(8,128)(2,1)}, s32[8,128]{1,0:T(8,128)}) custom-call(s32[128,128]{1,0:T(8,128)} %bitcast.11, s32[1,64]{1,0:T(1,128)} %bitcast.19), custom_call_target="tpu_custom_call" | custom-call | bytes 8388608 | tf_op jit(solution)/shard_map/pallas_call | solution.py:377
  20.7 0.3 all-to-all-done.got_ref
  21.0 0.0 copy-start
  21.0 4.5 %shard_map.119.acc_ref = f32[256,256]{1,0:T(8,128)S(1)} custom-call(f32[64,8,128]{2,1,0:T(8,128)S(1)} %all-to-all-done.got_ref), custom_call_target="tpu_custom_call" | custom-call | flops 4294967296 | bytes 524288 | tf_op jit(solution)/shard_map/pallas_call | solution.py:378
  25.5 0.0 copy-start.1
  25.5 0.0 copy-start.9
  25.5 0.0 copy-done.2
  25.5 0.0 copy-done.3
  25.5 0.0 copy-done.4
  25.5 0.0 copy-done.5
  25.5 0.0 copy-done.6
  25.6 0.0 copy-done.7
  25.6 0.0 copy-done.8
  25.6 0.0 copy-done
  25.6 2.4 %shard_map.121 = bf16[16,16,128]{2,1,0:T(8,128)(2,1)S(1)} custom-call(f32[256,256]{1,0:T(8,128)S(1)} %shard_map.119.acc_ref, s32[128,128]{1,0:T(8,128)S(1)} %bitcast.12, bf16[16,256,1024]{2,1,0:T(8,128)(2,1)S(1)} %copy-done, bf16[512,256]{1,0:T(8,128)(2,1)S(1)} %copy-done.4, bf16[512,256]{1,0:T(8,128)(2,1)S(1)} %copy-done.3, f32[256,128]{1,0:T(8,128)S(1)} %copy-done.6, ...), custom_call_target="tpu_custom_call" | custom-call | tf_op jit(solution)/shard_map/pallas_call | solution.py:385
  28.0 19.8 %all_to_all.15 = bf16[32,8,128]{2,1,0:T(8,128)(2,1)S(1)} all-to-all(bf16[32,8,128]{2,1,0:T(8,128)(2,1)S(1)} %bitcast.13), channel_id=1, replica_groups={{256,257,288,289,320,321,352,353,384,385,416,417,448,449,480,481,0,1,32..., dimensions={0} | all-to-all | bytes 131072 | tf_op jit(solution)/shard_map/all_to_all | solution.py:356
  47.8 0.1 shard_map.122
  47.9 8.8 %all_to_all.16 = f32[16,2,128]{2,1,0:T(2,128)S(1)} all-to-all(f32[16,2,128]{2,1,0:T(2,128)S(1)} %bitcast.16), channel_id=1, replica_groups={{20,22,24,26,28,30,0,2,4,6,8,10,12,14,16,18},{21,23,25,27,29,31,1,3,5,7..., dimensions={0} | all-to-all | bytes 32768 | tf_op jit(solution)/shard_map/all_to_all | solution.py:356
  56.8 0.0 copy-done.1
  56.8 0.0 copy-done.9
  56.8 1.2 %shard_map.123 = f32[64,128]{1,0:T(8,128)} custom-call(f32[32,128]{1,0:T(8,128)S(1)} %bitcast.15, s32[8,128]{1,0:T(8,128)S(1)} %copy-done.9, bf16[32,64,128]{2,1,0:T(8,128)(2,1)S(1)} %copy-done.1), custom_call_target="tpu_custom_call" | custom-call | tf_op jit(solution)/shard_map/pallas_call | solution.py:394
Async XLA Ops:
  0.0 25.5 %copy-start.2 = (s32[16384]{0:T(1024)S(1)}, s32[16384]{0:T(1024)}, u32[]{:S(2)}) copy-start(s32[16384]{0:T(1024)} %param.17) | copy-start | bytes 196612
  0.0 25.5 %copy-start.3 = (bf16[512,256]{1,0:T(8,128)(2,1)S(1)}, bf16[512,256]{1,0:T(8,128)(2,1)}, u32[]{:S(2)}) copy-start(bf16[512,256]{1,0:T(8,128)(2,1)} %constant.13.clone.one_l_ref) | copy-start | bytes 786436
  0.0 25.5 %copy-start.4 = (bf16[512,256]{1,0:T(8,128)(2,1)S(1)}, bf16[512,256]{1,0:T(8,128)(2,1)}, u32[]{:S(2)}) copy-start(bf16[512,256]{1,0:T(8,128)(2,1)} %constant.12.clone.one_h_ref) | copy-start | bytes 786436
  0.0 25.5 %copy-start.5 = (f32[256,128]{1,0:T(8,128)S(1)}, f32[256,128]{1,0:T(8,128)}, u32[]{:S(2)}) copy-start(f32[256,128]{1,0:T(8,128)} %constant.15.clone.sin_ref) | copy-start | bytes 393220
  0.0 25.5 %copy-start.6 = (f32[256,128]{1,0:T(8,128)S(1)}, f32[256,128]{1,0:T(8,128)}, u32[]{:S(2)}) copy-start(f32[256,128]{1,0:T(8,128)} %constant.14.clone.cos_ref) | copy-start | bytes 393220
  0.0 25.5 %copy-start.7 = (bf16[128,256]{1,0:T(8,128)(2,1)S(1)}, bf16[128,256]{1,0:T(8,128)(2,1)}, u32[]{:S(2)}) copy-start(bf16[128,256]{1,0:T(8,128)(2,1)} %constant.17.clone.two_l_ref) | copy-start | bytes 196612
  0.0 25.5 %copy-start.8 = (bf16[128,256]{1,0:T(8,128)(2,1)S(1)}, bf16[128,256]{1,0:T(8,128)(2,1)}, u32[]{:S(2)}) copy-start(bf16[128,256]{1,0:T(8,128)(2,1)} %constant.16.clone.two_h_ref) | copy-start | bytes 196612
  1.8 19.2 %all-to-all-start = ((f32[64,8,128]{2,1,0:T(8,128)}), f32[64,8,128]{2,1,0:T(8,128)S(1)}, u32[]{:S(2)}, u32[]{:S(2)}) async-start(f32[64,8,128]{2,1,0:T(8,128)} %bitcast.3), calls=%async_computation | async-start | bytes 524288 | tf_op jit(solution)/shard_map/all_to_all | solution.py:356
  21.0 4.6 %copy-start = (bf16[16,256,1024]{2,1,0:T(8,128)(2,1)S(1)}, bf16[16,256,1024]{2,1,0:T(8,128)(2,1)}, u32[]{:S(2)}) copy-start(bf16[16,256,1024]{2,1,0:T(8,128)(2,1)} %get-tuple-element.7.hits_ref) | copy-start | bytes 25165828
  25.5 31.3 %copy-start.1 = (bf16[32,64,128]{2,1,0:T(8,128)(2,1)S(1)}, bf16[32,64,128]{2,1,0:T(8,128)(2,1)}, u32[]{:S(2)}) copy-start(bf16[32,64,128]{2,1,0:T(8,128)(2,1)} %legendre_ref.1) | copy-start | bytes 1572868
  25.5 31.3 %copy-start.9 = (s32[8,128]{1,0:T(8,128)S(1)}, s32[8,128]{1,0:T(8,128)}, u32[]{:S(2)}) copy-start(s32[8,128]{1,0:T(8,128)} %get-tuple-element.8.side_ref) | copy-start | bytes 12292

commit v3 on v2

--- a/solution.py
+++ b/solution.py
@@ -21,7 +21,7 @@
 COLUMNS = (TILES + 1) * SUB
 
 FIRST_IN_BLOCK = 20
-FIRST_ON_LINE = 16
+FIRST_ON_LINE = 10
 FIRST_IN_PLANE = 10
 
 F32 = jnp.float32
@@ -159,32 +159,23 @@
     acc_ref[:, :COLUMNS] = deposit()
 
 
-def hits_kernel(
-    order_hbm, places_hbm, out_hbm, side_hbm, order_ref, places_ref, out_ref, side_ref, sems, block=None
+def spectrum_kernel(
+    acc_ref,
+    order_ref,
+    places_ref,
+    one_h_ref,
+    one_l_ref,
+    cos_ref,
+    sin_ref,
+    two_h_ref,
+    two_l_ref,
+    out_ref,
+    side_ref,
+    block=None,
 ):
     if block is None:
         block = lax.axis_index(("x", "core", "z_hi", "z_lo", "y"))
-    zero, one = jnp.zeros((), BF16), jnp.ones((), BF16)
-    planes = order_ref.shape[0] // 8
     cycles = places_ref.shape[1]
-    order_copy = pltpu.make_async_copy(order_hbm, order_ref, sems.at[planes])
-    places_copy = pltpu.make_async_copy(places_hbm, places_ref, sems.at[planes + 1])
-    side_copy = pltpu.make_async_copy(side_ref, side_hbm, sems.at[planes + 2])
-    out_copies = [
-        pltpu.make_async_copy(out_ref.at[k], out_hbm.at[k], sems.at[k]) for k in range(planes)
-    ]
-    order_copy.start()
-    places_copy.start()
-    order_copy.wait()
-    places_copy.wait()
-
-    ids = row_ids(ROWS)
-    for k in range(planes):
-        lower = (order_ref[pl.ds(k, 8, stride=planes), :] & (ROWS - 1)).astype(F32)
-        hits = [jnp.where(spread_row(lower, r, ROWS) == ids, one, zero) for r in range(8)]
-        out_ref[k] = jnp.concatenate(hits, axis=1)
-        out_copies[k].start()
-
     row = lax.broadcasted_iota(jnp.int32, (cycles, cycles), 0)
     column = lax.broadcasted_iota(jnp.int32, (cycles, cycles), 1)
     half = cycles // 2
@@ -195,15 +186,7 @@
     own = pltpu.roll(own, lax.rem(LANES + cycles - lax.rem(block, 4) * 32, LANES), 1)
     side_lane = lax.broadcasted_iota(jnp.int32, side_ref.shape, 1)
     side_ref[...] = jnp.where(side_lane < cycles, jnp.concatenate([places, places], axis=1), own)
-    side_copy.start()
-    for copy in out_copies:
-        copy.wait()
-    side_copy.wait()
-
-
-def spectrum_kernel(
-    acc_ref, order_ref, hits_ref, one_h_ref, one_l_ref, cos_ref, sin_ref, two_h_ref, two_l_ref, out_ref
-):
+
     beyond = acc_ref[:, LANES:]
     column = lax.broadcasted_iota(jnp.int32, (ROWS, LANES), 1)
     next_row = pltpu.roll(pltpu.roll(beyond, LANES - SUB + 1, 1), 1, 0)
@@ -227,11 +210,16 @@
         + dot(two_h_ref[...], twisted_h, NT)
     )
     spectrum = spectrum.astype(BF16)
+    zero, one = jnp.zeros((), BF16), jnp.ones((), BF16)
+    ids = row_ids(ROWS)
     upper_ids = lax.broadcasted_iota(jnp.int32, (UPPER, LANES), 0)
     planes = out_ref.shape[0]
     for k in range(planes):
-        upper = order_ref[pl.ds(k, 8, stride=planes), :] >> 8
-        picked = dot(spectrum, hits_ref[k], NN)
+        orders = order_ref[pl.ds(k, 8, stride=planes), :]
+        lower = (orders & (ROWS - 1)).astype(F32)
+        upper = orders >> 8
+        hits = [jnp.where(spread_row(lower, r, ROWS) == ids, one, zero) for r in range(8)]
+        picked = dot(spectrum, jnp.concatenate(hits, axis=1), NN)
         reals, imags = [], []
         for r in range(8):
             cols = slice(r * LANES, (r + 1) * LANES)
@@ -239,7 +227,7 @@
             reals.append(jnp.sum(jnp.where(mine, picked[:UPPER, cols], 0.0), axis=0, keepdims=True))
             imags.append(jnp.sum(jnp.where(mine, picked[UPPER:, cols], 0.0), axis=0, keepdims=True))
         rows = reals[::2] + imags[::2] + reals[1::2] + imags[1::2]
-        out_ref[(k - FIRST_ON_LINE // 2) % planes] = jnp.concatenate(rows, axis=0).astype(BF16)
+        out_ref[(FIRST_ON_LINE - k) % planes] = jnp.concatenate(rows, axis=0).astype(BF16)
 
 
 def slab_sum_kernel(parts_ref, out_ref):
@@ -326,33 +314,19 @@
     )
 
 
-def hits_call(planes, kernel=hits_kernel):
+def spectrum_call(planes, kernel=spectrum_kernel):
     outs = [
-        jax.ShapeDtypeStruct((planes, ROWS, M // planes), BF16),
+        jax.ShapeDtypeStruct((planes, 2 * M // planes // LANES, LANES), BF16),
         jax.ShapeDtypeStruct((8, LANES), jnp.int32),
     ]
-    cost = pl.CostEstimate(flops=0, transcendentals=0, bytes_accessed=2 * ROWS * M)
-    return kernel_call(
-        kernel,
-        outs,
-        None,
-        scratch=[
-            pltpu.VMEM((M // LANES, LANES), jnp.int32),
-            pltpu.VMEM((1, 64), jnp.int32),
-            pltpu.VMEM((planes, ROWS, M // planes), BF16),
-            pltpu.VMEM((8, LANES), jnp.int32),
-            pltpu.SemaphoreType.DMA((planes + 3,)),
-        ],
-        limit=60,
-        cost_estimate=cost,
-        in_specs=[pl.BlockSpec(memory_space=pl.ANY)] * 2,
-        out_specs=[pl.BlockSpec(memory_space=pl.ANY)] * 2,
-    )
-
-
-def exchange(values, axes, first):
-    count = lax.axis_size(axes)
-    members = [(first + n) % count for n in range(count)]
+    return kernel_call(kernel, outs, None)
+
+
+def members_from(first, count):
+    return [(first + n) % count for n in range(count)]
+
+
+def exchange(values, axes, members):
     return lax.all_to_all(
         values, axes, split_axis=0, concat_axis=0, axis_index_groups=[members], tiled=True
     )
@@ -373,8 +347,7 @@
     packed = pack_call(cycles, capacity)(
         *(pltpu.with_memory_space_constraint(value, pltpu.HBM) for value in particles)
     )
-    got = exchange(packed.reshape(cycles, 8, LANES), ("z_lo", "y", "x", "core"), FIRST_IN_BLOCK)
-    hits, side = hits_call(planes)(order_rows, cycle_order.reshape(1, cycles))
+    got = exchange(packed.reshape(cycles, 8, LANES), ("z_lo", "y", "x", "core"), members_from(FIRST_IN_BLOCK, cycles))
     cycle = kernel_call(
         deposit_kernel,
         (ROWS, 2 * LANES),
@@ -382,15 +355,16 @@
             flops=2 * cycles * capacity * ROWS * 2 * LANES, transcendentals=0, bytes_accessed=2**19
         ),
     )(got)
-    parts = kernel_call(spectrum_kernel, (planes, 2 * M // planes // LANES, LANES), BF16)(
-        cycle, order_rows, hits, *tables()
+    parts, side = spectrum_call(planes)(
+        cycle, order_rows, cycle_order.reshape(1, cycles), *tables()
     )
     parts = parts.reshape(2 * planes, M // planes // LANES, LANES)
-    got_parts = exchange(parts, z + ("core",), FIRST_ON_LINE)
+    line = [(FIRST_ON_LINE - n) % planes * 2 + core for n in range(planes) for core in range(2)]
+    got_parts = exchange(parts, z + ("core",), line)
     own = kernel_call(slab_sum_kernel, (cycles // 2, LANES), limit=4)(
         got_parts.reshape(planes, 2 * M // planes // LANES, LANES)
     )
-    spread = exchange(own.reshape(cycles // 4, 2, LANES), ("y", "x"), FIRST_IN_PLANE)
+    spread = exchange(own.reshape(cycles // 4, 2, LANES), ("y", "x"), members_from(FIRST_IN_PLANE, cycles // 4))
     alm = kernel_call(product_kernel, (2 * mode_count, LW), limit=8)(
         spread.reshape(cycles // 2, LANES), side, legendre
     )

time: 58.2 us -> 58.3 us (level)
  blocking collectives: 28.7 us -> 47.3 us
  starting transfers between devices: 14.5 us -> 0 us
  Pallas kernels: 14.3 us -> 9.67 us
    all_to_all x2 -> x3, blocking collectives: 28.7 us -> 47.3 us  [exchange(): lax.all_to_all(values, axes, split_axis=0, concat_axis=0, axis_index_grou...]
    all_to_all x1 -> x0, starting transfers between devices: 14.5 us -> none  [exchange(): lax.all_to_all(values, axes, split_axis=0, concat_axis=0, axis_index_grou...]
    pallas_call x2 -> x1, Pallas kernels: 6.77 us -> 2.94 us  [local(): spectrum_call(planes)]
    pallas_call x1, Pallas kernels: 1.74 us -> 0.97 us  [local(): pack_call(cycles, capacity)]
  transfers between devices with their start and end apart: 1 -> 0, of which waited for: 1 -> 0; matrix products, arithmetic and copies ran while one was open for 0% -> 0% of each run, Pallas kernels for 8% -> 0%
where the time goes in v3:
time: 58.3 us; the launch traced here: 57.7 us
  blocking collectives  47.3 us (81%)
  Pallas kernels  9.67 us (17%)
  local copies, waits for them, and re-layouts  0.62 us (1%)
    all_to_all x3, blocking collectives, exchange(): lax.all_to_all(values, axes, split_axis=0, concat_axis=0, axis_index_grou...  47.3 us
    pallas_call x1, Pallas kernels, local(): kernel_call(deposit_kernel, (ROWS, 2 * LANES), cost_estimate=pl.CostEstim...  4.5 us
    pallas_call x1, Pallas kernels, local(): spectrum_call(planes)  2.94 us
    pallas_call x1, Pallas kernels, local(): kernel_call(product_kernel, (2 * mode_count, LW), limit=8)  1.18 us

profile of v3, /device:TPU:1, one launch (start us, length us, event | category | flops | bytes accessed | tf_op | source)
XLA Modules:
  0.0 57.7 jit_solution(3197031194507126136)
XLA Ops:
  0.0 1.0 %shard_map.118 = f32[512,128]{1,0:T(8,128)S(1)} custom-call(f32[64,512]{1,0:T(8,128)} %bitcast.18, bf16[64,512]{1,0:T(8,128)(2,1)} %bitcast.19, s32[1,64]{1,0:T(1,128)} %bitcast.20), custom_call_target="tpu_custom_call" | custom-call | tf_op jit(solution)/shard_map/pallas_call | solution.py:347
  1.0 19.0 %all_to_all.15.got_ref = f32[64,8,128]{2,1,0:T(8,128)S(1)} all-to-all(f32[64,8,128]{2,1,0:T(8,128)S(1)} %bitcast.11), channel_id=1, replica_groups={{20,21,22,23,24,25,26,27,28,29,30,31,32,33,34,35,36,37,38,39,40,41,42,4..., dimensions={0} | all-to-all | bytes 524288 | tf_op jit(solution)/shard_map/all_to_all | solution.py:330
  19.9 0.0 copy-start.1
  19.9 0.0 copy-start.2
  19.9 0.0 copy-start.3
  19.9 0.0 copy-start.4
  20.0 0.0 copy-start.5
  20.0 0.0 copy-start.6
  20.0 0.0 copy-start.7
  20.0 4.5 %shard_map.119.acc_ref = f32[256,256]{1,0:T(8,128)S(1)} custom-call(f32[64,8,128]{2,1,0:T(8,128)S(1)} %all_to_all.15.got_ref), custom_call_target="tpu_custom_call" | custom-call | flops 4294967296 | bytes 524288 | tf_op jit(solution)/shard_map/pallas_call | solution.py:351
  24.5 0.0 copy-start.8
  24.5 0.0 copy-done.1
  24.5 0.0 copy-done.2
  24.5 0.0 copy-done.3
  24.5 0.0 copy-done.4
  24.5 0.0 copy-done.5
  24.6 0.0 copy-done.6
  24.6 0.0 copy-done.7
  24.6 0.6 copy-done.8
  25.2 0.0 copy-start
  25.2 2.9 %shard_map.120 = (bf16[16,16,128]{2,1,0:T(8,128)(2,1)S(1)}, s32[8,128]{1,0:T(8,128)S(1)}) custom-call(f32[256,256]{1,0:T(8,128)S(1)} %shard_map.119.acc_ref, s32[128,128]{1,0:T(8,128)S(1)} %bitcast.13, s32[1,64]{1,0:T(1,128)S(1)} %bitcast.17, bf16[512,256]{1,0:T(8,128)(2,1)S(1)} %copy-done.2, bf16[512,256]{1,0:T(8,128)(2,1)S(1)} %copy-done.1, ...), custom_call_target="tpu_custom_call" | custom-call | tf_op jit(solution)/shard_map/pallas_call | solution.py:358
  28.1 19.5 %all_to_all.16 = bf16[32,8,128]{2,1,0:T(8,128)(2,1)S(1)} all-to-all(bf16[32,8,128]{2,1,0:T(8,128)(2,1)S(1)} %bitcast.16), channel_id=1, replica_groups={{320,321,288,289,256,257,224,225,192,193,160,161,128,129,96,97,64,65,32..., dimensions={0} | all-to-all | bytes 131072 | tf_op jit(solution)/shard_map/all_to_all | solution.py:330
  47.6 0.1 shard_map.121
  47.7 8.8 %all_to_all.17 = f32[16,2,128]{2,1,0:T(2,128)S(1)} all-to-all(f32[16,2,128]{2,1,0:T(2,128)S(1)} %bitcast.15), channel_id=1, replica_groups={{20,22,24,26,28,30,0,2,4,6,8,10,12,14,16,18},{21,23,25,27,29,31,1,3,5,7..., dimensions={0} | all-to-all | bytes 32768 | tf_op jit(solution)/shard_map/all_to_all | solution.py:330
  56.5 0.0 copy-done
  56.5 1.2 %shard_map.122 = f32[64,128]{1,0:T(8,128)} custom-call(f32[32,128]{1,0:T(8,128)S(1)} %bitcast.14, s32[8,128]{1,0:T(8,128)S(1)} %get-tuple-element.8.side_ref, bf16[32,64,128]{2,1,0:T(8,128)(2,1)S(1)} %copy-done), custom_call_target="tpu_custom_call" | custom-call | tf_op jit(solution)/shard_map/pallas_call | solution.py:368
Async XLA Ops:
  19.9 4.6 %copy-start.1 = (bf16[512,256]{1,0:T(8,128)(2,1)S(1)}, bf16[512,256]{1,0:T(8,128)(2,1)}, u32[]{:S(2)}) copy-start(bf16[512,256]{1,0:T(8,128)(2,1)} %constant.13.clone.one_l_ref) | copy-start | bytes 786436
  19.9 4.6 %copy-start.2 = (bf16[512,256]{1,0:T(8,128)(2,1)S(1)}, bf16[512,256]{1,0:T(8,128)(2,1)}, u32[]{:S(2)}) copy-start(bf16[512,256]{1,0:T(8,128)(2,1)} %constant.12.clone.one_h_ref) | copy-start | bytes 786436
  19.9 4.6 %copy-start.3 = (f32[256,128]{1,0:T(8,128)S(1)}, f32[256,128]{1,0:T(8,128)}, u32[]{:S(2)}) copy-start(f32[256,128]{1,0:T(8,128)} %constant.15.clone.sin_ref) | copy-start | bytes 393220
  19.9 4.6 %copy-start.4 = (f32[256,128]{1,0:T(8,128)S(1)}, f32[256,128]{1,0:T(8,128)}, u32[]{:S(2)}) copy-start(f32[256,128]{1,0:T(8,128)} %constant.14.clone.cos_ref) | copy-start | bytes 393220
  20.0 4.6 %copy-start.5 = (s32[16384]{0:T(1024)S(1)}, s32[16384]{0:T(1024)}, u32[]{:S(2)}) copy-start(s32[16384]{0:T(1024)} %param.17) | copy-start | bytes 196612
  20.0 4.6 %copy-start.6 = (bf16[128,256]{1,0:T(8,128)(2,1)S(1)}, bf16[128,256]{1,0:T(8,128)(2,1)}, u32[]{:S(2)}) copy-start(bf16[128,256]{1,0:T(8,128)(2,1)} %constant.17.clone.two_l_ref) | copy-start | bytes 196612
  20.0 4.6 %copy-start.7 = (bf16[128,256]{1,0:T(8,128)(2,1)S(1)}, bf16[128,256]{1,0:T(8,128)(2,1)}, u32[]{:S(2)}) copy-start(bf16[128,256]{1,0:T(8,128)(2,1)} %constant.16.clone.two_h_ref) | copy-start | bytes 196612
  24.5 0.7 %copy-start.8 = (s32[64]{0:T(128)S(1)}, s32[64]{0:T(128)}, u32[]{:S(2)}) copy-start(s32[64]{0:T(128)} %param.16) | copy-start | bytes 772
  25.2 31.4 %copy-start = (bf16[32,64,128]{2,1,0:T(8,128)(2,1)S(1)}, bf16[32,64,128]{2,1,0:T(8,128)(2,1)}, u32[]{:S(2)}) copy-start(bf16[32,64,128]{2,1,0:T(8,128)(2,1)} %legendre_ref.1) | copy-start | bytes 1572868

commit v4 on v3

--- a/solution.py
+++ b/solution.py
@@ -162,7 +162,7 @@
 def spectrum_kernel(
     acc_ref,
     order_ref,
-    places_ref,
+    places_hbm,
     one_h_ref,
     one_l_ref,
     cos_ref,
@@ -171,21 +171,14 @@
     two_l_ref,
     out_ref,
     side_ref,
+    places_ref,
+    sems,
     block=None,
 ):
     if block is None:
         block = lax.axis_index(("x", "core", "z_hi", "z_lo", "y"))
-    cycles = places_ref.shape[1]
-    row = lax.broadcasted_iota(jnp.int32, (cycles, cycles), 0)
-    column = lax.broadcasted_iota(jnp.int32, (cycles, cycles), 1)
-    half = cycles // 2
-    taken = jnp.where(row == 2 * (column % half) + column // half, 1.0, 0.0).astype(BF16)
-    places = jnp.broadcast_to(places_ref[...], (16, cycles)).astype(F32).astype(BF16)
-    places = lax.dot_general(places, taken, NN, preferred_element_type=F32)[:8].astype(jnp.int32)
-    own = jnp.broadcast_to(order_ref[pl.ds(block // 4, 1), :], side_ref.shape)
-    own = pltpu.roll(own, lax.rem(LANES + cycles - lax.rem(block, 4) * 32, LANES), 1)
-    side_lane = lax.broadcasted_iota(jnp.int32, side_ref.shape, 1)
-    side_ref[...] = jnp.where(side_lane < cycles, jnp.concatenate([places, places], axis=1), own)
+    places_copy = pltpu.make_async_copy(places_hbm, places_ref, sems.at[0])
+    places_copy.start()
 
     beyond = acc_ref[:, LANES:]
     column = lax.broadcasted_iota(jnp.int32, (ROWS, LANES), 1)
@@ -229,6 +222,19 @@
         rows = reals[::2] + imags[::2] + reals[1::2] + imags[1::2]
         out_ref[(FIRST_ON_LINE - k) % planes] = jnp.concatenate(rows, axis=0).astype(BF16)
 
+    places_copy.wait()
+    cycles = places_ref.shape[1]
+    row = lax.broadcasted_iota(jnp.int32, (cycles, cycles), 0)
+    column = lax.broadcasted_iota(jnp.int32, (cycles, cycles), 1)
+    half = cycles // 2
+    taken = jnp.where(row == 2 * (column % half) + column // half, 1.0, 0.0).astype(BF16)
+    places = jnp.broadcast_to(places_ref[...], (16, cycles)).astype(F32).astype(BF16)
+    places = lax.dot_general(places, taken, NN, preferred_element_type=F32)[:8].astype(jnp.int32)
+    own = jnp.broadcast_to(order_ref[pl.ds(block // 4, 1), :], side_ref.shape)
+    own = pltpu.roll(own, lax.rem(LANES + cycles - lax.rem(block, 4) * 32, LANES), 1)
+    side_lane = lax.broadcasted_iota(jnp.int32, side_ref.shape, 1)
+    side_ref[...] = jnp.where(side_lane < cycles, jnp.concatenate([places, places], axis=1), own)
+
 
 def slab_sum_kernel(parts_ref, out_ref):
     z_count = parts_ref.shape[0]
@@ -319,7 +325,14 @@
         jax.ShapeDtypeStruct((planes, 2 * M // planes // LANES, LANES), BF16),
         jax.ShapeDtypeStruct((8, LANES), jnp.int32),
     ]
-    return kernel_call(kernel, outs, None)
+    whole, in_hbm = pl.BlockSpec(), pl.BlockSpec(memory_space=pl.ANY)
+    return kernel_call(
+        kernel,
+        outs,
+        None,
+        scratch=[pltpu.VMEM((1, 64), jnp.int32), pltpu.SemaphoreType.DMA((1,))],
+        in_specs=[whole, whole, in_hbm] + [whole] * 6,
+    )
 
 
 def members_from(first, count):
@@ -356,7 +369,10 @@
         ),
     )(got)
     parts, side = spectrum_call(planes)(
-        cycle, order_rows, cycle_order.reshape(1, cycles), *tables()
+        cycle,
+        order_rows,
+        pltpu.with_memory_space_constraint(cycle_order.reshape(1, cycles), pltpu.HBM),
+        *tables(),
     )
     parts = parts.reshape(2 * planes, M // planes // LANES, LANES)
     line = [(FIRST_ON_LINE - n) % planes * 2 + core for n in range(planes) for core in range(2)]

time: 58.3 us -> 58 us (level)
  no operation moved by 1% of the time
where the time goes in v4:
time: 58 us; the launch traced here: 57.4 us
  blocking collectives  47.3 us (82%)
  Pallas kernels  9.87 us (17%)
    all_to_all x3, blocking collectives, exchange(): lax.all_to_all(values, axes, split_axis=0, concat_axis=0, axis_index_grou...  47.3 us
    pallas_call x1, Pallas kernels, local(): kernel_call(deposit_kernel, (ROWS, 2 * LANES), cost_estimate=pl.CostEstim...  4.5 us
    pallas_call x1, Pallas kernels, local(): spectrum_call(planes)  3.14 us
    pallas_call x1, Pallas kernels, local(): kernel_call(product_kernel, (2 * mode_count, LW), limit=8)  1.17 us

profile of v4, /device:TPU:1, one launch (start us, length us, event | category | flops | bytes accessed | tf_op | source)
XLA Modules:
  0.0 57.4 jit_solution(13763224665532227808)
XLA Ops:
  0.0 1.0 %shard_map.118 = f32[512,128]{1,0:T(8,128)S(1)} custom-call(f32[64,512]{1,0:T(8,128)} %bitcast.17, bf16[64,512]{1,0:T(8,128)(2,1)} %bitcast.18, s32[1,64]{1,0:T(1,128)} %bitcast.20), custom_call_target="tpu_custom_call" | custom-call | tf_op jit(solution)/shard_map/pallas_call | solution.py:360
  1.0 19.0 %all_to_all.15.got_ref = f32[64,8,128]{2,1,0:T(8,128)S(1)} all-to-all(f32[64,8,128]{2,1,0:T(8,128)S(1)} %bitcast.11), channel_id=1, replica_groups={{20,21,22,23,24,25,26,27,28,29,30,31,32,33,34,35,36,37,38,39,40,41,42,4..., dimensions={0} | all-to-all | bytes 524288 | tf_op jit(solution)/shard_map/all_to_all | solution.py:343
  19.9 0.0 copy-start.1
  19.9 0.0 copy-start.2
  19.9 0.0 copy-start.3
  19.9 0.0 copy-start.4
  20.0 0.0 copy-start.5
  20.0 0.0 copy-start.6
  20.0 0.0 copy-start.7
  20.0 4.5 %shard_map.119.acc_ref = f32[256,256]{1,0:T(8,128)S(1)} custom-call(f32[64,8,128]{2,1,0:T(8,128)S(1)} %all_to_all.15.got_ref), custom_call_target="tpu_custom_call" | custom-call | flops 4294967296 | bytes 524288 | tf_op jit(solution)/shard_map/pallas_call | solution.py:364
  24.5 0.0 copy-done.1
  24.5 0.0 copy-done.2
  24.5 0.0 copy-done.3
  24.5 0.0 copy-done.4
  24.5 0.0 copy-done.5
  24.5 0.0 copy-done.6
  24.6 0.0 copy-done.7
  24.6 0.0 copy-start
  24.6 3.1 %shard_map.120 = (bf16[16,16,128]{2,1,0:T(8,128)(2,1)S(1)}, s32[8,128]{1,0:T(8,128)S(1)}) custom-call(f32[256,256]{1,0:T(8,128)S(1)} %shard_map.119.acc_ref, s32[128,128]{1,0:T(8,128)S(1)} %bitcast.13, s32[1,64]{1,0:T(1,128)} %bitcast.19, bf16[512,256]{1,0:T(8,128)(2,1)S(1)} %copy-done.2, bf16[512,256]{1,0:T(8,128)(2,1)S(1)} %copy-done.1, ...), custom_call_target="tpu_custom_call" | custom-call | tf_op jit(solution)/shard_map/pallas_call | solution.py:371
  27.7 19.5 %all_to_all.16 = bf16[32,8,128]{2,1,0:T(8,128)(2,1)S(1)} all-to-all(bf16[32,8,128]{2,1,0:T(8,128)(2,1)S(1)} %bitcast.16), channel_id=1, replica_groups={{320,321,288,289,256,257,224,225,192,193,160,161,128,129,96,97,64,65,32..., dimensions={0} | all-to-all | bytes 131072 | tf_op jit(solution)/shard_map/all_to_all | solution.py:343
  47.2 0.1 shard_map.121
  47.3 8.8 %all_to_all.17 = f32[16,2,128]{2,1,0:T(2,128)S(1)} all-to-all(f32[16,2,128]{2,1,0:T(2,128)S(1)} %bitcast.15), channel_id=1, replica_groups={{20,22,24,26,28,30,0,2,4,6,8,10,12,14,16,18},{21,23,25,27,29,31,1,3,5,7..., dimensions={0} | all-to-all | bytes 32768 | tf_op jit(solution)/shard_map/all_to_all | solution.py:343
  56.2 0.0 copy-done
  56.2 1.2 %shard_map.122 = f32[64,128]{1,0:T(8,128)} custom-call(f32[32,128]{1,0:T(8,128)S(1)} %bitcast.14, s32[8,128]{1,0:T(8,128)S(1)} %get-tuple-element.8.side_ref, bf16[32,64,128]{2,1,0:T(8,128)(2,1)S(1)} %copy-done), custom_call_target="tpu_custom_call" | custom-call | tf_op jit(solution)/shard_map/pallas_call | solution.py:384
Async XLA Ops:
  19.9 4.6 %copy-start.1 = (bf16[512,256]{1,0:T(8,128)(2,1)S(1)}, bf16[512,256]{1,0:T(8,128)(2,1)}, u32[]{:S(2)}) copy-start(bf16[512,256]{1,0:T(8,128)(2,1)} %constant.13.clone.one_l_ref) | copy-start | bytes 786436
  19.9 4.6 %copy-start.2 = (bf16[512,256]{1,0:T(8,128)(2,1)S(1)}, bf16[512,256]{1,0:T(8,128)(2,1)}, u32[]{:S(2)}) copy-start(bf16[512,256]{1,0:T(8,128)(2,1)} %constant.12.clone.one_h_ref) | copy-start | bytes 786436
  19.9 4.6 %copy-start.3 = (f32[256,128]{1,0:T(8,128)S(1)}, f32[256,128]{1,0:T(8,128)}, u32[]{:S(2)}) copy-start(f32[256,128]{1,0:T(8,128)} %constant.15.clone.sin_ref) | copy-start | bytes 393220
  19.9 4.6 %copy-start.4 = (f32[256,128]{1,0:T(8,128)S(1)}, f32[256,128]{1,0:T(8,128)}, u32[]{:S(2)}) copy-start(f32[256,128]{1,0:T(8,128)} %constant.14.clone.cos_ref) | copy-start | bytes 393220
  20.0 4.6 %copy-start.5 = (s32[16384]{0:T(1024)S(1)}, s32[16384]{0:T(1024)}, u32[]{:S(2)}) copy-start(s32[16384]{0:T(1024)} %param.17) | copy-start | bytes 196612
  20.0 4.6 %copy-start.6 = (bf16[128,256]{1,0:T(8,128)(2,1)S(1)}, bf16[128,256]{1,0:T(8,128)(2,1)}, u32[]{:S(2)}) copy-start(bf16[128,256]{1,0:T(8,128)(2,1)} %constant.17.clone.two_l_ref) | copy-start | bytes 196612
  20.0 4.6 %copy-start.7 = (bf16[128,256]{1,0:T(8,128)(2,1)S(1)}, bf16[128,256]{1,0:T(8,128)(2,1)}, u32[]{:S(2)}) copy-start(bf16[128,256]{1,0:T(8,128)(2,1)} %constant.16.clone.two_h_ref) | copy-start | bytes 196612
  24.6 31.6 %copy-start = (bf16[32,64,128]{2,1,0:T(8,128)(2,1)S(1)}, bf16[32,64,128]{2,1,0:T(8,128)(2,1)}, u32[]{:S(2)}) copy-start(bf16[32,64,128]{2,1,0:T(8,128)(2,1)} %legendre_ref.1) | copy-start | bytes 1572868
